TPU v7x, 32 devices: a whole 2x2x4 slice. The times are simulated.
32 devices in a mesh: shot: 2 (over y), depth: 2 (over core), lat: 8 (over z, x).
Axes of the slice: x: 2, y: 2, z: 4, core: 2. Of those that a mesh axis runs over, the one named last changes fastest.
Arguments:
- sources: float32 [6, 2, 32, 4096], P('shot', None, 'depth', 'lat'), parts along dimension 0, may hold values from -6 to 6
- blocks: float32 [4, 32, 7, 2, 128, 128], P(('shot', 'depth'), 'lat'), parts along dimension 0, may hold values from -0.125 to 0.125
- block_cols: int32 [2, 32, 7], P('depth', 'lat'), may hold values from 0 to 31, as said below
- refl_level: int32 [4096], P('lat'), may hold values from 0 to 1
- refl_coef: float32 [2, 4096], P(None, 'lat'), may hold values from -0.5 to 0.5
Outputs:
- bottom: float32 [6, 2, 32, 4096], P('shot', None, 'depth', 'lat'), parts along dimension 0
There are 2 independent parts, one for each index of `shot`. A program takes and returns all parts, laid end to end along the dimension named above; an argument that names none is the same for every part. Nothing has to cross between parts.
Inputs may be any that keep to these rules, and one draw needn't show every extreme that they name: block_cols[l, b, 0] = b, and every entry of row b lies within 4 block rows of b; a row may name a column twice.
All inputs are finite; a program needn't handle non-finite values.
Results may differ from a plain program's by a relative error of at most 0.0001.
Values sent between devices are 32-bit elements; how exact they have to be, the bound alone decides.
A program may use at most 64 MiB of HBM per device.

v0:
```python
import jax
import jax.numpy as jnp
from jax import lax
from jax.sharding import PartitionSpec as P


def extended(value, sides, width):
    for axis, dim in sides:
        devices, length = (lax.axis_size(axis), value.shape[dim])
        up = [(i, (i + 1) % devices) for i in range(devices - 1)]
        down = [(j, i) for i, j in up]
        last = lax.slice_in_dim(value, length - width, length, axis=dim)
        initial = lax.slice_in_dim(value, 0, width, axis=dim)
        before = lax.ppermute(last, axis, up)
        after = lax.ppermute(initial, axis, down)
        value = jnp.concatenate([before, value, after], axis=dim)
    return value


def per_device(sources, blocks, block_cols, refl_level, refl_coef):
    depth_count = lax.axis_size("depth")
    lat_pos = lax.axis_index("lat")
    panels = sources.shape[0]
    src_part = sources.shape[2]
    local_points = sources.shape[3]
    level_count = blocks.shape[0]
    block_rows = blocks.shape[1]
    per_row = blocks.shape[2]
    block_size = blocks.shape[4]
    shifted_base = (lat_pos - 1) * block_rows
    every_blocks, every_cols = (
        lax.all_gather(blocks, "depth", axis=0, tiled=True),
        lax.all_gather(block_cols, "depth", axis=0, tiled=True),
    )
    wavefield = jnp.transpose(sources, (1, 0, 2, 3)).reshape(2, panels * src_part, local_points)
    for level_global in range(depth_count * level_count):
        level_blocks = every_blocks[level_global]
        level_cols = every_cols[level_global]
        channels = wavefield.shape[1]
        at_level = refl_level == level_global
        coef_re = jnp.where(at_level, refl_coef[0], jnp.float32(0.0))
        coef_im = jnp.where(at_level, refl_coef[1], jnp.float32(0.0))
        field_re = wavefield[0]
        field_im = wavefield[1]
        combined = jnp.stack(
            [
                field_re + coef_re * field_re - coef_im * field_im,
                field_im + coef_re * field_im + coef_im * field_re,
            ]
        )
        widened = extended(combined, (("lat", 2),), local_points)
        stacked = widened.reshape(2 * channels, 3 * block_rows, block_size)
        local_cols = level_cols - shifted_base
        picked = jnp.take(stacked, local_cols.reshape(-1), axis=1)
        picked = picked.reshape(2 * channels, block_rows, per_row, block_size)
        real_part = jnp.einsum(
            "cbjp,bjpq->bcq", picked, level_blocks[:, :, 0], precision=lax.Precision.HIGHEST
        )
        imag_part = jnp.einsum(
            "cbjp,bjpq->bcq", picked, level_blocks[:, :, 1], precision=lax.Precision.HIGHEST
        )
        leaving_re = real_part[:, :channels] - imag_part[:, channels:]
        leaving_im = imag_part[:, :channels] + real_part[:, channels:]
        leaving = jnp.stack([leaving_re, leaving_im])
        wavefield = jnp.transpose(leaving, (0, 2, 1, 3)).reshape(2, channels, local_points)
    result = jnp.transpose(wavefield.reshape(2, panels, src_part, local_points), (1, 0, 2, 3))
    return result


def solution(mesh):
    placed = (
        P("shot", None, "depth", "lat"),
        P(("shot", "depth"), "lat", None, None, None, None),
        P("depth", "lat", None),
        P("lat"),
        P(None, "lat"),
    )
    return jax.shard_map(
        per_device,
        mesh=mesh,
        in_specs=placed,
        out_specs=P("shot", None, "depth", "lat"),
        check_vma=False,
    )
```

profile of v0, /device:TPU:10, one launch (start us, length us, event | category | flops | bytes accessed | tf_op | source)
XLA Modules:
  0.0 67.0 jit_solution(17550229805284339037)
XLA Ops:
  6.5 0.0 copy-start.2
  6.5 0.0 copy-start.4
  6.5 0.0 copy-start.1
  6.5 0.0 copy-start.3
  6.5 0.0 all-gather.2.cloned.1.call-start
  6.6 0.7 %all-gather.2.cloned.1.call-update = ((f32[1,4,7,2,128,128]{5,4,3,2,1,0:T(8,128)}), f32[2,4,7,2,128,128]{5,4,3,2,1,0:T(8,128)}) async-update(((), (), s32[]{:S(2)}) %all-gather.2.cloned.1.call-start, f32[1,4,7,2,128,128]{5,4,3,2,1,0:T(8,128)} %param.8) | async-update | bytes 14680088
  7.3 0.0 copy-done.2
  7.3 0.0 copy-done.4
  7.3 0.2 copy-done.1
  7.6 2.4 %collective-permute-start.1 = (f32[2,48,512]{2,1,0:T(8,128)S(1)}, f32[2,48,512]{2,1,0:T(8,128)S(1)}, u32[]{:S(2)}, u32[]{:S(2)}) collective-permute-start(f32[2,48,512]{2,1,0:T(8,128)S(1)} %pad_maximum_fusion.2), channel_id=1, source_target_pairs={{1,0},{2,1},{3,2},{4,3},{5,4},{6,5},{7,6},{9,8},{10,9},{11,10},{12... | collective-permute-start | bytes 589832 | tf_op jit(solution)/shard_map/ppermute | solution.py:15
  10.0 4.3 %collective-permute-start = (f32[2,48,512]{2,1,0:T(8,128)S(1)}, f32[2,48,512]{2,1,0:T(8,128)S(1)}, u32[]{:S(2)}, u32[]{:S(2)}) collective-permute-start(f32[2,48,512]{2,1,0:T(8,128)S(1)} %pad_maximum_fusion.2), channel_id=1, source_target_pairs={{0,1},{1,2},{2,3},{3,4},{4,5},{5,6},{6,7},{8,9},{9,10},{10,11},{11... | collective-permute-start | bytes 589832 | tf_op jit(solution)/shard_map/ppermute | solution.py:14
  14.3 0.0 copy-done.3
  14.3 1.8 %all_gather.6 = s32[2,4,7]{2,1,0:T(4,128)S(1)} all-gather(s32[1,4,7]{2,1,0:T(4,128)S(1)} %copy-done.3), channel_id=1, replica_groups=mesh['shot'=2,'depth'=2,'lat'=8] {'depth'}, dimensions={0}, use_global_device_ids=true | all-gather | bytes 336 | tf_op jit(solution)/shard_map/all_gather | solution.py:33
  16.1 0.1 sub.55
  16.2 0.1 sub.51
  16.4 2.1 %collective-permute-done.1 = f32[2,48,512]{2,1,0:T(8,128)S(1)} collective-permute-done((f32[2,48,512]{2,1,0:T(8,128)S(1)}, f32[2,48,512]{2,1,0:T(8,128)S(1)}, u32[]{:S(2)}, u32[]{:S(2)}) %collective-permute-start.1) | collective-permute-done | bytes 196640 | tf_op jit(solution)/shard_map/ppermute | solution.py:15
  18.4 2.8 %collective-permute-done = f32[2,48,512]{2,1,0:T(8,128)S(1)} collective-permute-done((f32[2,48,512]{2,1,0:T(8,128)S(1)}, f32[2,48,512]{2,1,0:T(8,128)S(1)}, u32[]{:S(2)}, u32[]{:S(2)}) %collective-permute-start) | collective-permute-done | bytes 196640 | tf_op jit(solution)/shard_map/ppermute | solution.py:14
  21.3 0.1 reshape.331
  21.4 0.2 copy.24
  21.6 0.6 gather_fusion
  22.2 0.2 broadcast_select_fusion.1
  22.4 6.3 %all-gather.2.cloned.1.call-done = f32[2,4,7,2,128,128]{5,4,3,2,1,0:T(8,128)} async-done(((f32[1,4,7,2,128,128]{5,4,3,2,1,0:T(8,128)}), f32[2,4,7,2,128,128]{5,4,3,2,1,0:T(8,128)}) %all-gather.2.cloned.1.call-update) | async-done | bytes 7340048 | tf_op jit(solution)/shard_map/all_gather | solution.py:32
  28.7 4.1 %fusion.16 = (f32[1,4,7,2,128,128]{5,4,3,2,1,0:T(8,128)S(1)}, f32[1,4,7,2,128,128]{5,4,3,2,1,0:T(8,128)S(1)}) fusion(f32[2,4,7,2,128,128]{5,4,3,2,1,0:T(8,128)} %all-gather.2.cloned.1.call-done), kind=kLoop, calls=%fused_computation.54 | loop fusion | bytes 14680064 | tf_op jit(solution)/shard_map/slice | solution.py:37
  32.8 2.7 %copy_bitcast_fusion = (f32[4,7,2,128,128]{4,3,1,0,2:T(8,128)}, f32[4,7,2,128,128]{4,3,1,0,2:T(8,128)S(1)}) fusion(f32[1,4,7,2,128,128]{5,4,3,2,1,0:T(8,128)S(1)} %get-tuple-element.10, f32[1,4,7,2,128,128]{5,4,3,2,1,0:T(8,128)S(1)} %get-tuple-element.11), kind=kLoop, calls=%fused_computation.2 | loop fusion | bytes 14680064 | tf_op jit(solution)/shard_map/squeeze | solution.py:37
  35.5 1.6 %fusion.5 = f32[4,96,128]{2,1,0:T(8,128)S(1)} fusion(f32[96,4,7,128]{3,0,2,1:T(8,128)S(1)} %bitcast.66, f32[4,7,2,128,128]{4,3,1,0,2:T(8,128)S(1)} %get-tuple-element.33), kind=kOutput, calls=%fused_computation.13 | convolution fusion | flops 528482304 | bytes 3407872 | tf_op jit(solution)/shard_map/cbjp,bjpq->bcq/dot_general | solution.py:59
  37.1 1.6 %fusion.4 = f32[4,96,128]{2,1,0:T(8,128)S(1)} fusion(f32[96,4,7,128]{3,0,2,1:T(8,128)S(1)} %bitcast.67, f32[4,7,2,128,128]{4,3,1,0,2:T(8,128)S(1)} %get-tuple-element.33), kind=kOutput, calls=%fused_computation.12 | convolution fusion | flops 528482304 | bytes 3407872 | tf_op jit(solution)/shard_map/cbjp,bjpq->bcq/dot_general | solution.py:56
  38.9 2.5 %collective-permute-start.3 = (f32[2,48,512]{2,1,0:T(8,128)S(1)}, f32[2,48,512]{2,1,0:T(8,128)S(1)}, u32[]{:S(2)}, u32[]{:S(2)}) collective-permute-start(f32[2,48,512]{2,1,0:T(8,128)S(1)} %pad_maximum_fusion.3), channel_id=1, source_target_pairs={{1,0},{2,1},{3,2},{4,3},{5,4},{6,5},{7,6},{9,8},{10,9},{11,10},{12... | collective-permute-start | bytes 589832 | tf_op jit(solution)/shard_map/ppermute | solution.py:15
  41.4 4.3 %collective-permute-start.2 = (f32[2,48,512]{2,1,0:T(8,128)S(1)}, f32[2,48,512]{2,1,0:T(8,128)S(1)}, u32[]{:S(2)}, u32[]{:S(2)}) collective-permute-start(f32[2,48,512]{2,1,0:T(8,128)S(1)} %pad_maximum_fusion.3), channel_id=1, source_target_pairs={{0,1},{1,2},{2,3},{3,4},{4,5},{5,6},{6,7},{8,9},{9,10},{10,11},{11... | collective-permute-start | bytes 589832 | tf_op jit(solution)/shard_map/ppermute | solution.py:14
  45.7 3.2 %collective-permute-done.3 = f32[2,48,512]{2,1,0:T(8,128)S(1)} collective-permute-done((f32[2,48,512]{2,1,0:T(8,128)S(1)}, f32[2,48,512]{2,1,0:T(8,128)S(1)}, u32[]{:S(2)}, u32[]{:S(2)}) %collective-permute-start.3) | collective-permute-done | bytes 196640 | tf_op jit(solution)/shard_map/ppermute | solution.py:15
  48.9 4.1 %collective-permute-done.2 = f32[2,48,512]{2,1,0:T(8,128)S(1)} collective-permute-done((f32[2,48,512]{2,1,0:T(8,128)S(1)}, f32[2,48,512]{2,1,0:T(8,128)S(1)}, u32[]{:S(2)}, u32[]{:S(2)}) %collective-permute-start.2) | collective-permute-done | bytes 196640 | tf_op jit(solution)/shard_map/ppermute | solution.py:14
  53.1 0.1 reshape.333
  53.2 0.2 copy.34
  53.4 0.6 gather_fusion.1
  54.0 0.0 copy-start
  54.1 0.2 broadcast_select_fusion
  54.2 3.3 %fusion.7 = f32[4,96,128]{2,1,0:T(8,128)S(1)} fusion(f32[96,4,7,128]{3,0,2,1:T(8,128)S(1)} %bitcast.68, f32[4,7,2,128,128]{4,3,1,0,2:T(8,128)} %get-tuple-element.32), kind=kOutput, calls=%fused_computation.15 | convolution fusion | flops 528482304 | bytes 3407872 | tf_op jit(solution)/shard_map/cbjp,bjpq->bcq/dot_general | solution.py:59
  57.5 0.0 copy-done
  57.5 1.6 %fusion.6 = f32[4,96,128]{2,1,0:T(8,128)S(1)} fusion(f32[96,4,7,128]{3,0,2,1:T(8,128)S(1)} %bitcast.69, f32[4,7,2,128,128]{4,3,1,0,2:T(8,128)S(1)} %copy-done), kind=kOutput, calls=%fused_computation.14 | convolution fusion | flops 528482304 | bytes 3407872 | tf_op jit(solution)/shard_map/cbjp,bjpq->bcq/dot_general | solution.py:56
  59.2 0.1 copy.36
  59.3 0.1 reshape_reshape.3
  59.4 0.7 %copy.37 = f32[3,2,16,512]{3,2,1,0:T(8,128)} copy(f32[3,2,16,512]{3,2,0,1:T(8,128)S(1)} %bitcast.70) | data formatting | bytes 393216 | tf_op jit(solution)/shard_map/transpose | solution.py:66
  (24 shorter events, 0.4 us)
Async XLA Ops:
  6.5 0.7 %copy-start.2 = (f32[2,512]{1,0:T(2,128)S(1)}, f32[2,512]{1,0:T(2,128)}, u32[]{:S(2)}) copy-start(f32[2,512]{1,0:T(2,128)} %param.11) | copy-start | bytes 12292
  6.5 0.8 %copy-start.4 = (s32[512]{0:T(512)S(1)}, s32[512]{0:T(512)}, u32[]{:S(2)}) copy-start(s32[512]{0:T(512)} %param.10) | copy-start | bytes 6148
  6.5 1.0 %copy-start.1 = (f32[3,2,16,512]{3,2,1,0:T(8,128)S(1)}, f32[3,2,16,512]{3,2,1,0:T(8,128)}, u32[]{:S(2)}) copy-start(f32[3,2,16,512]{3,2,1,0:T(8,128)} %param.7) | copy-start | bytes 589828
  6.5 7.8 %copy-start.3 = (s32[1,4,7]{2,1,0:T(4,128)S(1)}, s32[1,4,7]{2,1,0:T(4,128)}, u32[]{:S(2)}) copy-start(s32[1,4,7]{2,1,0:T(4,128)} %param.9) | copy-start | bytes 340
  6.5 22.1 %all-gather.2.cloned.1.call-start = ((), (), s32[]{:S(2)}) async-start(), calls=%async_computation | async-start | bytes 11010048 | tf_op jit(solution)/shard_map/all_gather | solution.py:32
  7.6 10.8 %collective-permute-start.1 = (f32[2,48,512]{2,1,0:T(8,128)S(1)}, f32[2,48,512]{2,1,0:T(8,128)S(1)}, u32[]{:S(2)}, u32[]{:S(2)}) collective-permute-start(f32[2,48,512]{2,1,0:T(8,128)S(1)} %pad_maximum_fusion.2), channel_id=1, source_target_pairs={{1,0},{2,1},{3,2},{4,3},{5,4},{6,5},{7,6},{9,8},{10,9},{11,10},{12... | collective-permute-start | bytes 589832 | tf_op jit(solution)/shard_map/ppermute | solution.py:15
  10.0 11.2 %collective-permute-start = (f32[2,48,512]{2,1,0:T(8,128)S(1)}, f32[2,48,512]{2,1,0:T(8,128)S(1)}, u32[]{:S(2)}, u32[]{:S(2)}) collective-permute-start(f32[2,48,512]{2,1,0:T(8,128)S(1)} %pad_maximum_fusion.2), channel_id=1, source_target_pairs={{0,1},{1,2},{2,3},{3,4},{4,5},{5,6},{6,7},{8,9},{9,10},{10,11},{11... | collective-permute-start | bytes 589832 | tf_op jit(solution)/shard_map/ppermute | solution.py:14
  38.9 10.0 %collective-permute-start.3 = (f32[2,48,512]{2,1,0:T(8,128)S(1)}, f32[2,48,512]{2,1,0:T(8,128)S(1)}, u32[]{:S(2)}, u32[]{:S(2)}) collective-permute-start(f32[2,48,512]{2,1,0:T(8,128)S(1)} %pad_maximum_fusion.3), channel_id=1, source_target_pairs={{1,0},{2,1},{3,2},{4,3},{5,4},{6,5},{7,6},{9,8},{10,9},{11,10},{12... | collective-permute-start | bytes 589832 | tf_op jit(solution)/shard_map/ppermute | solution.py:15
  41.4 11.6 %collective-permute-start.2 = (f32[2,48,512]{2,1,0:T(8,128)S(1)}, f32[2,48,512]{2,1,0:T(8,128)S(1)}, u32[]{:S(2)}, u32[]{:S(2)}) collective-permute-start(f32[2,48,512]{2,1,0:T(8,128)S(1)} %pad_maximum_fusion.3), channel_id=1, source_target_pairs={{0,1},{1,2},{2,3},{3,4},{4,5},{5,6},{6,7},{8,9},{9,10},{10,11},{11... | collective-permute-start | bytes 589832 | tf_op jit(solution)/shard_map/ppermute | solution.py:14
  54.0 3.5 %copy-start = (f32[4,7,2,128,128]{4,3,1,0,2:T(8,128)S(1)}, f32[4,7,2,128,128]{4,3,1,0,2:T(8,128)}, u32[]{:S(2)}) copy-start(f32[4,7,2,128,128]{4,3,1,0,2:T(8,128)} %get-tuple-element.32) | copy-start | bytes 11010052
Sparse Core Ops, SparseCore 0:
  8.9 19.6 all-gather.1
where the time goes:
time: 67.7 us; the launch traced here: 67 us
  waiting for transfers between devices  19.1 us (28%)
  between operations  13.7 us (20%)
  starting transfers between devices  13.5 us (20%)
  local copies, waits for them, and re-layouts  10 us (15%)
  matrix products  8.14 us (12%)
  blocking collectives  1.78 us (3%)
    ppermute x2, starting transfers between devices, extended(): before = lax.ppermute(last, axis, up)  8.58 us
    ppermute x2, waiting for transfers between devices, extended(): before = lax.ppermute(last, axis, up)  6.92 us
    all_gather x1, waiting for transfers between devices, per_device(): lax.all_gather(blocks, 'depth', axis=0, tiled=True)  6.26 us
    ppermute x2, waiting for transfers between devices, extended(): after = lax.ppermute(initial, axis, down)  5.28 us
    ppermute x2, starting transfers between devices, extended(): after = lax.ppermute(initial, axis, down)  4.91 us
    dot_general x2, matrix products, per_device(): jnp.einsum('cbjp,bjpq->bcq', picked, level_blocks[:, :, 1], precision=lax...  4.89 us
    slice x1, local copies, waits for them, and re-layouts, per_device(): level_blocks = every_blocks[level_global]  4.09 us
    dot_general x2, matrix products, per_device(): jnp.einsum('cbjp,bjpq->bcq', picked, level_blocks[:, :, 0], precision=lax...  3.24 us
  transfers between devices with their start and end apart: 5, of which 5 were waited for; matrix products, arithmetic and copies ran while one was open for 2% of the time, Pallas kernels for 0%

commit v1 on v0

v1 whole, which is shorter than its diff:
```python
import functools

import jax
import jax.numpy as jnp
from jax import lax
from jax.experimental import pallas as pl
from jax.experimental.pallas import tpu as pltpu
from jax.sharding import PartitionSpec as P

MESH = pl.DeviceIdType.MESH


def split_bf16(value):
    high = value.astype(jnp.bfloat16)
    low = (value - high.astype(jnp.float32)).astype(jnp.bfloat16)
    return high, low


def kernel(
    lat_count, blocks, cols, sources, level, coef, out,
    raw, w_hi, w_lo, src, lev, cf, entering, field, parts, stage, final,
    load_w, load_s, load_r,
    send_c, send_x, send_z, send_cx, send_cc, send_o,
    recv_c, recv_x, recv_z, recv_o, store_o,
):
    panels, _, part, points = sources.shape
    _, rows, per_row, _, size, _ = blocks.shape
    half = 2 * part
    depth = lax.axis_index("depth")
    lat = lax.axis_index("lat")
    odd = lax.rem(lat, 2)
    pair = lat + 1 - 2 * odd
    onward = lat + 2 - 4 * odd
    behind = lat - 2 + 4 * odd
    has_onward = jnp.logical_and(onward >= 0, onward < lat_count)
    has_behind = jnp.logical_and(behind >= 0, behind < lat_count)
    near = 2 * rows * (1 - odd)
    far = 2 * rows * odd

    weight_loads = [
        pltpu.make_async_copy(blocks.at[0, b], raw.at[b], load_w.at[b]) for b in range(rows)
    ]
    source_loads = [
        pltpu.make_async_copy(sources.at[k], src.at[k], load_s.at[k]) for k in range(panels)
    ]
    refl_loads = [
        pltpu.make_async_copy(level, lev, load_r.at[0]),
        pltpu.make_async_copy(coef, cf, load_r.at[1]),
    ]
    for copy in refl_loads + source_loads + weight_loads:
        copy.start()

    barrier = pltpu.get_barrier_semaphore()
    pl.semaphore_signal(barrier, device_id={"depth": 1 - depth, "lat": lat}, device_id_type=MESH)
    pl.semaphore_signal(barrier, device_id={"depth": 1 - depth, "lat": pair}, device_id_type=MESH)

    @pl.when(depth == 0)
    def _():
        pl.semaphore_signal(barrier, device_id={"depth": 0, "lat": pair}, device_id_type=MESH)

    @pl.when(has_behind)
    def _():
        pl.semaphore_signal(barrier, device_id={"depth": depth, "lat": behind}, device_id_type=MESH)

    for copy in refl_loads:
        copy.wait()

    def coefficients(at):
        here = lev[...] == at
        zero = jnp.float32(0.0)
        return jnp.where(here, cf[0:1, :], zero), jnp.where(here, cf[1:2, :], zero)

    def reflected(re, im, c_re, c_im):
        return re + c_re * re - c_im * im, im + c_re * im + c_im * re

    def send(src_ref, dst_ref, send_sem, recv_sem, to_depth, to_lat):
        return pltpu.make_async_remote_copy(
            src_ref=src_ref, dst_ref=dst_ref, send_sem=send_sem, recv_sem=recv_sem,
            device_id={"depth": to_depth, "lat": to_lat}, device_id_type=MESH,
        )

    def entering_across(k):
        return send(
            entering.at[k], field.at[k, depth, pl.ds(far, rows)],
            send_x.at[k], recv_x.at[k, depth], 0, pair,
        )

    def entering_own(k):
        return send(
            entering.at[k], field.at[k, 1, pl.ds(rows, rows)],
            send_c.at[k], recv_c.at[k, 1], 0, lat,
        )

    def leaving_across(k, d):
        return send(
            stage.at[k, d], field.at[k, d, pl.ds(far, rows)],
            send_cx.at[k, d], recv_x.at[k, d], 1, pair,
        )

    def leaving_own(k, d):
        return send(
            stage.at[k, d], field.at[k, d, pl.ds(rows, rows)],
            send_cc.at[k, d], recv_c.at[k, d], 1, lat,
        )

    def onward_copy(k, d):
        return send(
            field.at[k, d, pl.ds(near, rows)], field.at[k, d, pl.ds(far, rows)],
            send_z.at[k, d], recv_z.at[k, d], depth, onward,
        )

    def return_copy(k):
        return send(final.at[k, 0], out.at[k], send_o.at[k], recv_o.at[k], 0, lat)

    c_re, c_im = coefficients(0)
    for k in range(panels):
        source_loads[k].wait()
        for b in range(rows):
            at = slice(b * size, (b + 1) * size)
            re, im = reflected(src[k, 0, :, at], src[k, 1, :, at], c_re[:, at], c_im[:, at])
            entering[k, b, 0:part] = re
            entering[k, b, part:half] = im

            @pl.when(depth == 0)
            def _():
                field[k, 0, rows + b, 0:part] = re
                field[k, 0, rows + b, part:half] = im

        if k == 0:
            pl.semaphore_wait(barrier, 3 - depth + has_onward.astype(jnp.int32))
        entering_across(k).start()

        @pl.when(depth == 1)
        def _():
            entering_own(k).start()

    for b in range(rows):
        weight_loads[b].wait()

        @pl.loop(0, per_row)
        def _(j):
            for c in range(2):
                high, low = split_bf16(raw[b, j, c])
                at = pl.ds(pl.multiple_of(j * size, size), size)
                w_hi[b, at, c * size:(c + 1) * size] = high
                w_lo[b, at, c * size:(c + 1) * size] = low

    def pass_on(k):
        for d in range(2):
            leaving_across(k, d).wait_recv()

            @pl.when(has_onward)
            def _():
                onward_copy(k, d).start()

    c_re, c_im = coefficients(1)
    base = (lat - 1) * rows
    pass_on(0)
    for k in range(panels):
        if k + 1 < panels:
            pass_on(k + 1)

        @pl.when(depth == 1)
        def _():
            leaving_own(k, 0).wait_recv()

        leaving_own(k, 1).wait_recv()

        @pl.when(has_behind)
        def _():
            for d in range(2):
                onward_copy(k, d).wait_recv()

        for slot in range(3 * rows):
            for d in range(2):
                high, low = split_bf16(field[k, d, slot])
                parts[k, slot, d * half:(d + 1) * half] = high
                parts[k, slot, (2 + d) * half:(3 + d) * half] = low

        for b in range(rows):
            picked = jnp.concatenate(
                [parts[k, jnp.clip(cols[0, b, j] - base, 0, 3 * rows - 1)] for j in range(per_row)],
                axis=1,
            )
            both = jnp.dot(picked, w_hi[b], preferred_element_type=jnp.float32)
            rest = jnp.dot(picked[:2 * half], w_lo[b], preferred_element_type=jnp.float32)
            total = both[:2 * half] + (both[2 * half:] + rest)
            at = slice(b * size, (b + 1) * size)
            leaving = []
            for d in range(2):
                of_re = total[d * half:d * half + part]
                of_im = total[d * half + part:(d + 1) * half]
                leaving.append(
                    (of_re[:, :size] - of_im[:, size:], of_re[:, size:] + of_im[:, :size])
                )

            @pl.when(depth == 0)
            def _():
                for d in range(2):
                    re, im = reflected(*leaving[d], c_re[:, at], c_im[:, at])
                    stage[k, d, b, 0:part] = re
                    stage[k, d, b, part:half] = im

            @pl.when(depth == 1)
            def _():
                for d in range(2):
                    for c in range(2):
                        final[k, d, c, :, at] = leaving[d][c]

        @pl.when(depth == 0)
        def _():
            for d in range(2):
                leaving_across(k, d).start()
            for d in range(2):
                leaving_own(k, d).start()

        @pl.when(depth == 1)
        def _():
            return_copy(k).start()
            pltpu.make_async_copy(final.at[k, 1], out.at[k], store_o.at[k]).start()

    @pl.when(depth == 0)
    def _():
        for k in range(panels):
            for d in range(2):
                leaving_across(k, d).wait_send()
                leaving_own(k, d).wait_send()
            return_copy(k).wait_recv()

    @pl.when(depth == 1)
    def _():
        for k in range(panels):
            entering_own(k).wait_send()
            return_copy(k).wait_send()
            pltpu.make_async_copy(final.at[k, 1], out.at[k], store_o.at[k]).wait()

    for k in range(panels):
        entering_across(k).wait_send()

    @pl.when(has_onward)
    def _():
        for k in range(panels):
            for d in range(2):
                onward_copy(k, d).wait_send()


def per_device(sources, blocks, block_cols, refl_level, refl_coef):
    lat_count = lax.axis_size("lat")
    assert lax.axis_size("depth") == 2 and blocks.shape[0] == 1 and lat_count % 2 == 0
    panels, _, part, points = sources.shape
    _, rows, per_row, _, size, _ = blocks.shape
    half = 2 * part
    f32, bf16 = jnp.float32, jnp.bfloat16
    dma = pltpu.SemaphoreType.DMA
    anywhere = pl.BlockSpec(memory_space=pl.ANY)
    flops = 2 * 3 * 4 * panels * part * 2 * rows * per_row * size * size * 2
    return pl.pallas_call(
        functools.partial(kernel, lat_count),
        out_shape=jax.ShapeDtypeStruct(sources.shape, f32),
        in_specs=[
            anywhere,
            pl.BlockSpec(memory_space=pltpu.SMEM),
            anywhere,
            anywhere,
            anywhere,
        ],
        out_specs=anywhere,
        scratch_shapes=[
            pltpu.VMEM((rows, per_row, 2, size, size), f32),
            pltpu.VMEM((rows, per_row * size, 2 * size), bf16),
            pltpu.VMEM((rows, per_row * size, 2 * size), bf16),
            pltpu.VMEM((panels, 2, part, points), f32),
            pltpu.VMEM((1, points), jnp.int32),
            pltpu.VMEM((2, points), f32),
            pltpu.VMEM((panels, rows, half, size), f32),
            pltpu.VMEM((panels, 2, 3 * rows, half, size), f32),
            pltpu.VMEM((panels, 3 * rows, 4 * half, size), bf16),
            pltpu.VMEM((panels, 2, rows, half, size), f32),
            pltpu.VMEM((panels, 2, 2, part, points), f32),
            dma((rows,)), dma((panels,)), dma((2,)),
            dma((panels,)), dma((panels,)), dma((panels, 2)),
            dma((panels, 2)), dma((panels, 2)), dma((panels,)),
            dma((panels, 2)), dma((panels, 2)), dma((panels, 2)),
            dma((panels,)), dma((panels,)),
        ],
        compiler_params=pltpu.CompilerParams(
            collective_id=0, has_side_effects=True, vmem_limit_bytes=63 * 1024 * 1024
        ),
        cost_estimate=pl.CostEstimate(
            flops=flops, bytes_accessed=4 * (blocks.size + 2 * sources.size), transcendentals=0
        ),
    )(blocks, block_cols, sources, refl_level.reshape(1, points), refl_coef)


def solution(mesh):
    placed = (
        P("shot", None, "depth", "lat"),
        P(("shot", "depth"), "lat", None, None, None, None),
        P("depth", "lat", None),
        P("lat"),
        P(None, "lat"),
    )
    return jax.shard_map(
        per_device,
        mesh=mesh,
        in_specs=placed,
        out_specs=P("shot", None, "depth", "lat"),
        check_vma=False,
    )
```

time: 67.7 us -> 30.2 us (0.45)
  the two profiles are of different devices: /device:TPU:10 before, /device:TPU:0 now
where the time goes in v1:
time: 30.2 us; the launch traced here: 30.1 us
  Pallas kernels  28.4 us (94%)
  local copies, waits for them, and re-layouts  1.62 us (5%)
    pallas_call x1, Pallas kernels, per_device(): pl.pallas_call(functools.partial(kernel, lat_count), out_shape=jax.ShapeD...  28.4 us
    unnamed x1, local copies, waits for them, and re-layouts  1.62 us

profile of v1, /device:TPU:0, one launch (start us, length us, event | category | flops | bytes accessed | tf_op | source)
XLA Modules:
  0.0 30.1 jit_solution(13909548252078132165)
XLA Ops:
  0.0 28.4 %shard_map.55 = f32[3,2,16,512]{3,2,1,0:T(8,128)} custom-call(f32[1,4,7,2,128,128]{5,4,3,2,1,0:T(8,128)} %blocks.1, s32[1,4,7]{2,1,0:T(4,128)} %cols.1, f32[3,2,16,512]{3,2,1,0:T(8,128)} %sources.1, s32[1,512]{1,0:T(1,128)} %bitcast.1, f32[2,512]{1,0:T(2,128)} %coef.1), custom_call_target="tpu_custom_call" | custom-call | flops 2113929216 | bytes 4063232 | tf_op jit(solution)/shard_map/pallas_call | solution.py:257
  28.5 1.6 %copy.7 = f32[3,2,16,512]{3,2,1,0:T(8,128)} copy(f32[3,2,16,512]{3,2,1,0:T(8,128)} %shard_map.55) | data formatting | bytes 393216

commit v2 on v1

--- a/solution.py
+++ b/solution.py
@@ -112,6 +112,15 @@
     def return_copy(k):
         return send(final.at[k, 0], out.at[k], send_o.at[k], recv_o.at[k], 0, lat)
 
+    def send_entering(k):
+        if k > 0:
+            entering_across(k - 1).wait_send()
+        entering_across(k).start()
+
+        @pl.when(depth == 1)
+        def _():
+            entering_own(k).start()
+
     c_re, c_im = coefficients(0)
     for k in range(panels):
         source_loads[k].wait()
@@ -128,11 +137,7 @@
 
         if k == 0:
             pl.semaphore_wait(barrier, 3 - depth + has_onward.astype(jnp.int32))
-        entering_across(k).start()
-
-        @pl.when(depth == 1)
-        def _():
-            entering_own(k).start()
+            send_entering(0)
 
     for b in range(rows):
         weight_loads[b].wait()
@@ -155,10 +160,16 @@
 
     c_re, c_im = coefficients(1)
     base = (lat - 1) * rows
-    pass_on(0)
     for k in range(panels):
+        if k == 0 and panels > 1:
+            send_entering(1)
+            pass_on(0)
+        if k + 2 < panels:
+            send_entering(k + 2)
         if k + 1 < panels:
             pass_on(k + 1)
+        if panels == 1:
+            pass_on(0)
 
         @pl.when(depth == 1)
         def _():
@@ -234,8 +245,7 @@
             return_copy(k).wait_send()
             pltpu.make_async_copy(final.at[k, 1], out.at[k], store_o.at[k]).wait()
 
-    for k in range(panels):
-        entering_across(k).wait_send()
+    entering_across(panels - 1).wait_send()
 
     @pl.when(has_onward)
     def _():

time: 30.2 us -> 35.3 us (1.17)
  Pallas kernels: 28.4 us -> 33.5 us
    pallas_call x1, Pallas kernels: 28.4 us -> 33.5 us  [per_device(): pl.pallas_call(functools.partial(kernel, lat_count), out_shape=jax.ShapeD...]
where the time goes in v2:
time: 35.3 us; the launch traced here: 35.2 us
  Pallas kernels  33.5 us (95%)
  local copies, waits for them, and re-layouts  1.62 us (5%)
    pallas_call x1, Pallas kernels, per_device(): pl.pallas_call(functools.partial(kernel, lat_count), out_shape=jax.ShapeD...  33.5 us
    unnamed x1, local copies, waits for them, and re-layouts  1.62 us

profile of v2, /device:TPU:0, one launch (start us, length us, event | category | flops | bytes accessed | tf_op | source)
XLA Modules:
  0.0 35.2 jit_solution(17541402933959046286)
XLA Ops:
  0.0 33.5 %shard_map.55 = f32[3,2,16,512]{3,2,1,0:T(8,128)} custom-call(f32[1,4,7,2,128,128]{5,4,3,2,1,0:T(8,128)} %blocks.1, s32[1,4,7]{2,1,0:T(4,128)} %cols.1, f32[3,2,16,512]{3,2,1,0:T(8,128)} %sources.1, s32[1,512]{1,0:T(1,128)} %bitcast.1, f32[2,512]{1,0:T(2,128)} %coef.1), custom_call_target="tpu_custom_call" | custom-call | flops 2113929216 | bytes 4063232 | tf_op jit(solution)/shard_map/pallas_call | solution.py:267
  33.5 1.6 %copy.7 = f32[3,2,16,512]{3,2,1,0:T(8,128)} copy(f32[3,2,16,512]{3,2,1,0:T(8,128)} %shard_map.55) | data formatting | bytes 393216

commit v3 on v0

v3 whole, which is shorter than its diff:
```python
import functools

import jax
import jax.numpy as jnp
from jax import lax
from jax.experimental import pallas as pl
from jax.experimental.pallas import tpu as pltpu
from jax.sharding import PartitionSpec as P

MESH = pl.DeviceIdType.MESH


def split_bf16(value):
    high = value.astype(jnp.bfloat16)
    low = (value - high.astype(jnp.float32)).astype(jnp.bfloat16)
    return high, low


def kernel(
    lat_count, blocks, cols, cols_hbm, sources, level, coef, out,
    raw, w_hi, w_lo, src, lev, cf, field, parts, final, cols_in, cols_other,
    load_w, load_s, load_r, load_c, send_w, recv_w, send_i, recv_i,
    send_x, recv_x, send_z, recv_z, store_o,
):
    panels, _, part, points = sources.shape
    _, rows, per_row, _, size, _ = blocks.shape
    half = panels * part
    full = 2 * half
    depth = lax.axis_index("depth")
    lat = lax.axis_index("lat")
    odd = lax.rem(lat, 2)
    pair = lat + 1 - 2 * odd
    onward = lat + 2 - 4 * odd
    behind = lat - 2 + 4 * odd
    has_onward = jnp.logical_and(onward >= 0, onward < lat_count)
    has_behind = jnp.logical_and(behind >= 0, behind < lat_count)
    near = 2 * rows * (1 - odd)
    far = 2 * rows * odd

    weight_loads = [
        pltpu.make_async_copy(blocks.at[0, b], raw.at[depth, b], load_w.at[b])
        for b in range(rows)
    ]
    source_load = pltpu.make_async_copy(sources, src, load_s.at[0])
    refl_loads = [
        pltpu.make_async_copy(level, lev, load_r.at[0]),
        pltpu.make_async_copy(coef, cf, load_r.at[1]),
    ]
    for copy in refl_loads + [source_load] + weight_loads:
        copy.start()

    barrier = pltpu.get_barrier_semaphore()
    pl.semaphore_signal(barrier, device_id={"depth": 1 - depth, "lat": lat}, device_id_type=MESH)
    pl.semaphore_signal(barrier, device_id={"depth": depth, "lat": pair}, device_id_type=MESH)

    @pl.when(has_behind)
    def _():
        pl.semaphore_signal(barrier, device_id={"depth": depth, "lat": behind}, device_id_type=MESH)

    for copy in refl_loads:
        copy.wait()

    def coefficients(at):
        here = lev[...] == at
        zero = jnp.float32(0.0)
        return jnp.where(here, cf[0:1, :], zero), jnp.where(here, cf[1:2, :], zero)

    def reflected(re, im, c_re, c_im):
        return re + c_re * re - c_im * im, im + c_re * im + c_im * re

    def send(src_ref, dst_ref, send_sem, recv_sem, to_depth, to_lat):
        return pltpu.make_async_remote_copy(
            src_ref=src_ref, dst_ref=dst_ref, send_sem=send_sem, recv_sem=recv_sem,
            device_id={"depth": to_depth, "lat": to_lat}, device_id_type=MESH,
        )

    def across(l, b):
        return send(
            field.at[l, rows + b], field.at[l, far + b],
            send_x.at[l, b], recv_x.at[l, b], depth, pair,
        )

    def along(l, b):
        return send(
            field.at[l, near + b], field.at[l, far + b],
            send_z.at[l, b], recv_z.at[l, b], depth, onward,
        )

    def exchange(b):
        return send(
            blocks.at[0, b], raw.at[depth, b], send_w.at[b], recv_w.at[b], 1 - depth, lat,
        )

    def exchange_cols():
        return send(cols_hbm, cols_in, send_i.at[0], recv_i.at[0], 1 - depth, lat)

    def split_slot(l, slot):
        high, low = split_bf16(field[l, slot])
        parts[slot, 0:full] = high
        parts[slot, full:2 * full] = low

    def split_row(l, b):
        @pl.loop(0, per_row)
        def _(j):
            at = pl.ds(pl.multiple_of(j * size, size), size)
            for c in range(2):
                high, low = split_bf16(raw[l, b, j, c])
                w_hi[l, b, at, c * size:(c + 1) * size] = high
                w_lo[l, b, at, c * size:(c + 1) * size] = low

    def split_received(l, own):
        @pl.when(depth != own)
        def _():
            for b in range(rows):
                exchange(b).wait_recv()
                split_row(l, b)

    def finish_halo(l):
        for b in range(rows):
            split_slot(l, rows + b)
            split_slot(l, near + b)

        @pl.when(has_behind)
        def _():
            for b in range(rows):
                along(l, b).wait_recv()
                split_slot(l, far + b)

    def pass_on(l, b):
        across(l, b).wait_recv()

        @pl.when(has_onward)
        def _():
            along(l, b).start()

    base = (lat - 1) * rows

    def column(l, b, j):
        listed = jnp.where(depth == l, cols[0, b, j], cols_other[0, b, j])
        return jnp.clip(listed - base, 0, 3 * rows - 1)

    def row_of(l, b):
        picked = jnp.concatenate([parts[column(l, b, j)] for j in range(per_row)], axis=1)
        both = jnp.dot(picked, w_hi[l, b], preferred_element_type=jnp.float32)
        rest = jnp.dot(picked[:full], w_lo[l, b], preferred_element_type=jnp.float32)
        total = both[:full] + (both[full:] + rest)
        of_re, of_im = total[:half], total[half:]
        return of_re[:, :size] - of_im[:, size:], of_re[:, size:] + of_im[:, :size]

    c_re, c_im = coefficients(0)
    source_load.wait()
    for b in range(rows):
        at = slice(b * size, (b + 1) * size)
        for k in range(panels):
            re, im = reflected(src[k, 0, :, at], src[k, 1, :, at], c_re[:, at], c_im[:, at])
            field[0, rows + b, k * part:(k + 1) * part] = re
            field[0, rows + b, half + k * part:half + (k + 1) * part] = im
        if b == 0:
            pl.semaphore_wait(barrier, 2 + has_onward.astype(jnp.int32))
        across(0, b).start()
    exchange_cols().start()
    for b in range(rows):
        exchange(b).start()

    for b in range(rows):
        weight_loads[b].wait()
        split_row(depth, b)
        pass_on(0, b)
    exchange_cols().wait_recv()
    listed = pltpu.make_async_copy(cols_in, cols_other, load_c.at[0])
    listed.start()
    finish_halo(0)
    split_received(0, 0)
    listed.wait()

    c_re, c_im = coefficients(1)
    for b in range(rows):
        at = slice(b * size, (b + 1) * size)
        re, im = reflected(*row_of(0, b), c_re[:, at], c_im[:, at])
        field[1, rows + b, 0:half] = re
        field[1, rows + b, half:full] = im
        across(1, b).start()
    split_received(1, 1)
    for b in range(rows):
        pass_on(1, b)
    finish_halo(1)
    for b in range(rows):
        at = slice(b * size, (b + 1) * size)
        re, im = row_of(1, b)
        for k in range(panels):
            final[k, 0, :, at] = re[k * part:(k + 1) * part]
            final[k, 1, :, at] = im[k * part:(k + 1) * part]
    store = pltpu.make_async_copy(final, out, store_o.at[0])
    store.start()

    exchange_cols().wait_send()
    for b in range(rows):
        exchange(b).wait_send()
        for l in range(2):
            across(l, b).wait_send()

    @pl.when(has_onward)
    def _():
        for l in range(2):
            for b in range(rows):
                along(l, b).wait_send()

    store.wait()


def per_device(sources, blocks, block_cols, refl_level, refl_coef):
    lat_count = lax.axis_size("lat")
    assert lax.axis_size("depth") == 2 and blocks.shape[0] == 1 and lat_count % 2 == 0
    panels, _, part, points = sources.shape
    _, rows, per_row, _, size, _ = blocks.shape
    full = 2 * panels * part
    f32, bf16 = jnp.float32, jnp.bfloat16
    dma = pltpu.SemaphoreType.DMA
    anywhere = pl.BlockSpec(memory_space=pl.ANY)
    flops = 2 * 3 * 2 * full * rows * per_row * size * size * 2
    return pl.pallas_call(
        functools.partial(kernel, lat_count),
        out_shape=jax.ShapeDtypeStruct(sources.shape, f32),
        in_specs=[
            anywhere,
            pl.BlockSpec(memory_space=pltpu.SMEM),
            anywhere,
            anywhere,
            anywhere,
            anywhere,
        ],
        out_specs=anywhere,
        scratch_shapes=[
            pltpu.VMEM((2, rows, per_row, 2, size, size), f32),
            pltpu.VMEM((2, rows, per_row * size, 2 * size), bf16),
            pltpu.VMEM((2, rows, per_row * size, 2 * size), bf16),
            pltpu.VMEM((panels, 2, part, points), f32),
            pltpu.VMEM((1, points), jnp.int32),
            pltpu.VMEM((2, points), f32),
            pltpu.VMEM((2, 3 * rows, full, size), f32),
            pltpu.VMEM((3 * rows, 2 * full, size), bf16),
            pltpu.VMEM((panels, 2, part, points), f32),
            pltpu.VMEM(block_cols.shape, jnp.int32),
            pltpu.SMEM(block_cols.shape, jnp.int32),
            dma((rows,)), dma((1,)), dma((2,)), dma((1,)),
            dma((rows,)), dma((rows,)), dma((1,)), dma((1,)),
            dma((2, rows)), dma((2, rows)), dma((2, rows)), dma((2, rows)), dma((1,)),
        ],
        compiler_params=pltpu.CompilerParams(
            collective_id=0, has_side_effects=True, vmem_limit_bytes=63 * 1024 * 1024
        ),
        cost_estimate=pl.CostEstimate(
            flops=flops, bytes_accessed=4 * (blocks.size + 2 * sources.size), transcendentals=0
        ),
    )(blocks, block_cols, block_cols, sources, refl_level.reshape(1, points), refl_coef)


def solution(mesh):
    placed = (
        P("shot", None, "depth", "lat"),
        P(("shot", "depth"), "lat", None, None, None, None),
        P("depth", "lat", None),
        P("lat"),
        P(None, "lat"),
    )
    return jax.shard_map(
        per_device,
        mesh=mesh,
        in_specs=placed,
        out_specs=P("shot", None, "depth", "lat"),
        check_vma=False,
    )
```

time: 67.7 us -> 24.8 us (0.37)
  Pallas kernels: 0 us -> 23 us
  waiting for transfers between devices: 19.1 us -> 0 us
  between operations: 13.7 us -> 0.01 us
  starting transfers between devices: 13.5 us -> 0 us
  local copies, waits for them, and re-layouts: 10 us -> 1.62 us
  matrix products: 8.14 us -> 0 us
  blocking collectives: 1.78 us -> 0 us
    pallas_call x0 -> x1, Pallas kernels: none -> 23 us  [per_device(): pl.pallas_call(functools.partial(kernel, lat_count), out_shape=jax.ShapeD...]
    ppermute x4 -> x0, starting transfers between devices: 13.5 us -> none  [the longest x2 8.58 us: extended(): before = lax.ppermute(last, axis, up)]
    ppermute x4 -> x0, waiting for transfers between devices: 12.2 us -> none  [the longest x2 6.92 us: extended(): before = lax.ppermute(last, axis, up)]
    dot_general x4 -> x0, matrix products: 8.14 us -> none  [the longest x2 4.89 us: per_device(): jnp.einsum('cbjp,bjpq->bcq', picked, level_blocks[:, :, 1], precision=lax...]
    all_gather x1 -> x0, waiting for transfers between devices: 6.26 us -> none  [per_device(): lax.all_gather(blocks, 'depth', axis=0, tiled=True)]
    slice x6 -> x0, local copies, waits for them, and re-layouts: 4.21 us -> none  [the longest x1 4.09 us: per_device(): level_blocks = every_blocks[level_global]]
    squeeze x1 -> x0, local copies, waits for them, and re-layouts: 2.74 us -> none  [per_device(): level_blocks = every_blocks[level_global]]
    all_gather x1 -> x0, blocking collectives: 1.78 us -> none  [per_device(): lax.all_gather(block_cols, 'depth', axis=0, tiled=True)]
  transfers between devices with their start and end apart: 5 -> 0, of which waited for: 5 -> 0; matrix products, arithmetic and copies ran while one was open for 2% -> 0% of each run, Pallas kernels for 0% -> 0%
where the time goes in v3:
time: 24.8 us; the launch traced here: 24.6 us
  Pallas kernels  23 us (93%)
  local copies, waits for them, and re-layouts  1.62 us (7%)
    pallas_call x1, Pallas kernels, per_device(): pl.pallas_call(functools.partial(kernel, lat_count), out_shape=jax.ShapeD...  23 us
    unnamed x1, local copies, waits for them, and re-layouts  1.62 us

profile of v3, /device:TPU:10, one launch (start us, length us, event | category | flops | bytes accessed | tf_op | source)
XLA Modules:
  0.0 24.6 jit_solution(8353839272977374502)
XLA Ops:
  0.0 23.0 %shard_map.55 = f32[3,2,16,512]{3,2,1,0:T(8,128)} custom-call(f32[1,4,7,2,128,128]{5,4,3,2,1,0:T(8,128)} %blocks.1, s32[1,4,7]{2,1,0:T(4,128)} %cols_hbm.1, s32[1,4,7]{2,1,0:T(4,128)} %cols_hbm.1, f32[3,2,16,512]{3,2,1,0:T(8,128)} %sources.1, s32[1,512]{1,0:T(1,128)} %bitcast.1, f32[2,512]{1,0:T(2,128)} %coef.1), custom_call_target="tpu_custom_call" | custom-call | flops 1056964608 | bytes 4063232 | tf_op jit(solution)/shard_map/pallas_call | solution.py:221
  23.0 1.6 %copy.7 = f32[3,2,16,512]{3,2,1,0:T(8,128)} copy(f32[3,2,16,512]{3,2,1,0:T(8,128)} %shard_map.55) | data formatting | bytes 393216

commit v4 on v3

--- a/solution.py
+++ b/solution.py
@@ -20,18 +20,20 @@
     lat_count, blocks, cols, cols_hbm, sources, level, coef, out,
     raw, w_hi, w_lo, src, lev, cf, field, parts, final, cols_in, cols_other,
     load_w, load_s, load_r, load_c, send_w, recv_w, send_i, recv_i,
-    send_x, recv_x, send_z, recv_z, store_o,
+    send_x, recv_x, send_z, recv_z, send_d, store_o,
 ):
     panels, _, part, points = sources.shape
     _, rows, per_row, _, size, _ = blocks.shape
     half = panels * part
     full = 2 * half
+    relayed = rows - 1
     depth = lax.axis_index("depth")
     lat = lax.axis_index("lat")
     odd = lax.rem(lat, 2)
     pair = lat + 1 - 2 * odd
     onward = lat + 2 - 4 * odd
     behind = lat - 2 + 4 * odd
+    diagonal = lat - 1 + 2 * odd
     has_onward = jnp.logical_and(onward >= 0, onward < lat_count)
     has_behind = jnp.logical_and(behind >= 0, behind < lat_count)
     near = 2 * rows * (1 - odd)
@@ -56,6 +58,9 @@
     @pl.when(has_behind)
     def _():
         pl.semaphore_signal(barrier, device_id={"depth": depth, "lat": behind}, device_id_type=MESH)
+        pl.semaphore_signal(
+            barrier, device_id={"depth": depth, "lat": diagonal}, device_id_type=MESH
+        )
 
     for copy in refl_loads:
         copy.wait()
@@ -86,6 +91,20 @@
             send_z.at[l, b], recv_z.at[l, b], depth, onward,
         )
 
+    def direct(l, b):
+        return send(
+            field.at[l, rows + b], field.at[l, near + b],
+            send_d.at[l, b - relayed], recv_z.at[l, b], depth, diagonal,
+        )
+
+    def start_halo(l, b):
+        across(l, b).start()
+        if b >= relayed:
+
+            @pl.when(has_behind)
+            def _():
+                direct(l, b).start()
+
     def exchange(b):
         return send(
             blocks.at[0, b], raw.at[depth, b], send_w.at[b], recv_w.at[b], 1 - depth, lat,
@@ -96,8 +115,8 @@
 
     def split_slot(l, slot):
         high, low = split_bf16(field[l, slot])
-        parts[slot, 0:full] = high
-        parts[slot, full:2 * full] = low
+        parts[l, slot, 0:full] = high
+        parts[l, slot, full:2 * full] = low
 
     def split_row(l, b):
         @pl.loop(0, per_row)
@@ -108,18 +127,13 @@
                 w_hi[l, b, at, c * size:(c + 1) * size] = high
                 w_lo[l, b, at, c * size:(c + 1) * size] = low
 
-    def split_received(l, own):
+    def split_received(l, b, own):
         @pl.when(depth != own)
         def _():
-            for b in range(rows):
-                exchange(b).wait_recv()
-                split_row(l, b)
+            exchange(b).wait_recv()
+            split_row(l, b)
 
     def finish_halo(l):
-        for b in range(rows):
-            split_slot(l, rows + b)
-            split_slot(l, near + b)
-
         @pl.when(has_behind)
         def _():
             for b in range(rows):
@@ -128,10 +142,13 @@
 
     def pass_on(l, b):
         across(l, b).wait_recv()
-
-        @pl.when(has_onward)
-        def _():
-            along(l, b).start()
+        if b < relayed:
+
+            @pl.when(has_onward)
+            def _():
+                along(l, b).start()
+
+        split_slot(l, near + b)
 
     base = (lat - 1) * rows
 
@@ -140,7 +157,7 @@
         return jnp.clip(listed - base, 0, 3 * rows - 1)
 
     def row_of(l, b):
-        picked = jnp.concatenate([parts[column(l, b, j)] for j in range(per_row)], axis=1)
+        picked = jnp.concatenate([parts[l, column(l, b, j)] for j in range(per_row)], axis=1)
         both = jnp.dot(picked, w_hi[l, b], preferred_element_type=jnp.float32)
         rest = jnp.dot(picked[:full], w_lo[l, b], preferred_element_type=jnp.float32)
         total = both[:full] + (both[full:] + rest)
@@ -156,12 +173,14 @@
             field[0, rows + b, k * part:(k + 1) * part] = re
             field[0, rows + b, half + k * part:half + (k + 1) * part] = im
         if b == 0:
-            pl.semaphore_wait(barrier, 2 + has_onward.astype(jnp.int32))
-        across(0, b).start()
+            pl.semaphore_wait(barrier, 2 + has_onward.astype(jnp.int32) + has_behind.astype(jnp.int32))
+        start_halo(0, b)
     exchange_cols().start()
     for b in range(rows):
         exchange(b).start()
 
+    for b in range(rows):
+        split_slot(0, rows + b)
     for b in range(rows):
         weight_loads[b].wait()
         split_row(depth, b)
@@ -169,9 +188,10 @@
     exchange_cols().wait_recv()
     listed = pltpu.make_async_copy(cols_in, cols_other, load_c.at[0])
     listed.start()
+    for b in range(rows):
+        split_received(0, b, 0)
+    listed.wait()
     finish_halo(0)
-    split_received(0, 0)
-    listed.wait()
 
     c_re, c_im = coefficients(1)
     for b in range(rows):
@@ -179,9 +199,11 @@
         re, im = reflected(*row_of(0, b), c_re[:, at], c_im[:, at])
         field[1, rows + b, 0:half] = re
         field[1, rows + b, half:full] = im
-        across(1, b).start()
-    split_received(1, 1)
-    for b in range(rows):
+        start_halo(1, b)
+    for b in range(rows):
+        split_slot(1, rows + b)
+    for b in range(rows):
+        split_received(1, b, 1)
         pass_on(1, b)
     finish_halo(1)
     for b in range(rows):
@@ -202,8 +224,14 @@
     @pl.when(has_onward)
     def _():
         for l in range(2):
-            for b in range(rows):
+            for b in range(relayed):
                 along(l, b).wait_send()
+
+    @pl.when(has_behind)
+    def _():
+        for l in range(2):
+            for b in range(relayed, rows):
+                direct(l, b).wait_send()
 
     store.wait()
 
@@ -238,13 +266,13 @@
             pltpu.VMEM((1, points), jnp.int32),
             pltpu.VMEM((2, points), f32),
             pltpu.VMEM((2, 3 * rows, full, size), f32),
-            pltpu.VMEM((3 * rows, 2 * full, size), bf16),
+            pltpu.VMEM((2, 3 * rows, 2 * full, size), bf16),
             pltpu.VMEM((panels, 2, part, points), f32),
             pltpu.VMEM(block_cols.shape, jnp.int32),
             pltpu.SMEM(block_cols.shape, jnp.int32),
             dma((rows,)), dma((1,)), dma((2,)), dma((1,)),
             dma((rows,)), dma((rows,)), dma((1,)), dma((1,)),
-            dma((2, rows)), dma((2, rows)), dma((2, rows)), dma((2, rows)), dma((1,)),
+            dma((2, rows)), dma((2, rows)), dma((2, rows)), dma((2, rows)), dma((2, rows)), dma((1,)),
         ],
         compiler_params=pltpu.CompilerParams(
             collective_id=0, has_side_effects=True, vmem_limit_bytes=63 * 1024 * 1024

time: 24.8 us -> 25 us (level)
    pallas_call x1, Pallas kernels: 23 us -> 23.2 us  [per_device(): pl.pallas_call(functools.partial(kernel, lat_count), out_shape=jax.ShapeD...]
where the time goes in v4:
time: 25 us; the launch traced here: 24.9 us
  Pallas kernels  23.2 us (93%)
  local copies, waits for them, and re-layouts  1.62 us (6%)
    pallas_call x1, Pallas kernels, per_device(): pl.pallas_call(functools.partial(kernel, lat_count), out_shape=jax.ShapeD...  23.2 us
    unnamed x1, local copies, waits for them, and re-layouts  1.62 us

profile of v4, /device:TPU:10, one launch (start us, length us, event | category | flops | bytes accessed | tf_op | source)
XLA Modules:
  0.0 24.9 jit_solution(6327279868837942381)
XLA Ops:
  0.0 23.2 %shard_map.55 = f32[3,2,16,512]{3,2,1,0:T(8,128)} custom-call(f32[1,4,7,2,128,128]{5,4,3,2,1,0:T(8,128)} %blocks.1, s32[1,4,7]{2,1,0:T(4,128)} %cols_hbm.1, s32[1,4,7]{2,1,0:T(4,128)} %cols_hbm.1, f32[3,2,16,512]{3,2,1,0:T(8,128)} %sources.1, s32[1,512]{1,0:T(1,128)} %bitcast.1, f32[2,512]{1,0:T(2,128)} %coef.1), custom_call_target="tpu_custom_call" | custom-call | flops 1056964608 | bytes 4063232 | tf_op jit(solution)/shard_map/pallas_call | solution.py:249
  23.2 1.6 %copy.7 = f32[3,2,16,512]{3,2,1,0:T(8,128)} copy(f32[3,2,16,512]{3,2,1,0:T(8,128)} %shard_map.55) | data formatting | bytes 393216

commit v5 on v4

--- a/solution.py
+++ b/solution.py
@@ -119,19 +119,16 @@
         parts[l, slot, full:2 * full] = low
 
     def split_row(l, b):
-        @pl.loop(0, per_row)
-        def _(j):
-            at = pl.ds(pl.multiple_of(j * size, size), size)
+        for j in range(per_row):
+            at = slice(j * size, (j + 1) * size)
             for c in range(2):
                 high, low = split_bf16(raw[l, b, j, c])
                 w_hi[l, b, at, c * size:(c + 1) * size] = high
                 w_lo[l, b, at, c * size:(c + 1) * size] = low
 
-    def split_received(l, b, own):
-        @pl.when(depth != own)
-        def _():
-            exchange(b).wait_recv()
-            split_row(l, b)
+    def split_received(b):
+        exchange(b).wait_recv()
+        split_row(1 - depth, b)
 
     def finish_halo(l):
         @pl.when(has_behind)
@@ -184,12 +181,22 @@
     for b in range(rows):
         weight_loads[b].wait()
         split_row(depth, b)
+        if b >= rows // 2:
+            pass_on(0, b - rows // 2)
+    early = rows // 2
+    for b in range(rows - rows // 2, rows):
         pass_on(0, b)
+    for b in range(early):
+        split_received(b)
     exchange_cols().wait_recv()
     listed = pltpu.make_async_copy(cols_in, cols_other, load_c.at[0])
     listed.start()
-    for b in range(rows):
-        split_received(0, b, 0)
+
+    @pl.when(depth == 1)
+    def _():
+        for b in range(early, rows):
+            split_received(b)
+
     listed.wait()
     finish_halo(0)
 
@@ -202,8 +209,13 @@
         start_halo(1, b)
     for b in range(rows):
         split_slot(1, rows + b)
-    for b in range(rows):
-        split_received(1, b, 1)
+
+    @pl.when(depth == 0)
+    def _():
+        for b in range(early, rows):
+            split_received(b)
+
+    for b in range(rows):
         pass_on(1, b)
     finish_halo(1)
     for b in range(rows):

time: 25 us -> 25 us (level)
  no operation moved by 1% of the time
where the time goes in v5:
time: 25 us; the launch traced here: 24.9 us
  Pallas kernels  23.2 us (93%)
  local copies, waits for them, and re-layouts  1.62 us (6%)
    pallas_call x1, Pallas kernels, per_device(): pl.pallas_call(functools.partial(kernel, lat_count), out_shape=jax.ShapeD...  23.2 us
    unnamed x1, local copies, waits for them, and re-layouts  1.62 us

profile of v5, /device:TPU:10, one launch (start us, length us, event | category | flops | bytes accessed | tf_op | source)
XLA Modules:
  0.0 24.9 jit_solution(489824067572019407)
XLA Ops:
  0.0 23.2 %shard_map.55 = f32[3,2,16,512]{3,2,1,0:T(8,128)} custom-call(f32[1,4,7,2,128,128]{5,4,3,2,1,0:T(8,128)} %blocks.1, s32[1,4,7]{2,1,0:T(4,128)} %cols_hbm.1, s32[1,4,7]{2,1,0:T(4,128)} %cols_hbm.1, f32[3,2,16,512]{3,2,1,0:T(8,128)} %sources.1, s32[1,512]{1,0:T(1,128)} %bitcast.1, f32[2,512]{1,0:T(2,128)} %coef.1), custom_call_target="tpu_custom_call" | custom-call | flops 1056964608 | bytes 4063232 | tf_op jit(solution)/shard_map/pallas_call | solution.py:261
  23.2 1.6 %copy.7 = f32[3,2,16,512]{3,2,1,0:T(8,128)} copy(f32[3,2,16,512]{3,2,1,0:T(8,128)} %shard_map.55) | data formatting | bytes 393216

commit v6 on v5

--- a/solution.py
+++ b/solution.py
@@ -20,20 +20,18 @@
     lat_count, blocks, cols, cols_hbm, sources, level, coef, out,
     raw, w_hi, w_lo, src, lev, cf, field, parts, final, cols_in, cols_other,
     load_w, load_s, load_r, load_c, send_w, recv_w, send_i, recv_i,
-    send_x, recv_x, send_z, recv_z, send_d, store_o,
+    send_x, recv_x, send_z, recv_z, store_o,
 ):
     panels, _, part, points = sources.shape
     _, rows, per_row, _, size, _ = blocks.shape
     half = panels * part
     full = 2 * half
-    relayed = rows - 1
     depth = lax.axis_index("depth")
     lat = lax.axis_index("lat")
     odd = lax.rem(lat, 2)
     pair = lat + 1 - 2 * odd
     onward = lat + 2 - 4 * odd
     behind = lat - 2 + 4 * odd
-    diagonal = lat - 1 + 2 * odd
     has_onward = jnp.logical_and(onward >= 0, onward < lat_count)
     has_behind = jnp.logical_and(behind >= 0, behind < lat_count)
     near = 2 * rows * (1 - odd)
@@ -58,9 +56,6 @@
     @pl.when(has_behind)
     def _():
         pl.semaphore_signal(barrier, device_id={"depth": depth, "lat": behind}, device_id_type=MESH)
-        pl.semaphore_signal(
-            barrier, device_id={"depth": depth, "lat": diagonal}, device_id_type=MESH
-        )
 
     for copy in refl_loads:
         copy.wait()
@@ -90,20 +85,6 @@
             field.at[l, near + b], field.at[l, far + b],
             send_z.at[l, b], recv_z.at[l, b], depth, onward,
         )
-
-    def direct(l, b):
-        return send(
-            field.at[l, rows + b], field.at[l, near + b],
-            send_d.at[l, b - relayed], recv_z.at[l, b], depth, diagonal,
-        )
-
-    def start_halo(l, b):
-        across(l, b).start()
-        if b >= relayed:
-
-            @pl.when(has_behind)
-            def _():
-                direct(l, b).start()
 
     def exchange(b):
         return send(
@@ -139,11 +120,10 @@
 
     def pass_on(l, b):
         across(l, b).wait_recv()
-        if b < relayed:
-
-            @pl.when(has_onward)
-            def _():
-                along(l, b).start()
+
+        @pl.when(has_onward)
+        def _():
+            along(l, b).start()
 
         split_slot(l, near + b)
 
@@ -170,8 +150,8 @@
             field[0, rows + b, k * part:(k + 1) * part] = re
             field[0, rows + b, half + k * part:half + (k + 1) * part] = im
         if b == 0:
-            pl.semaphore_wait(barrier, 2 + has_onward.astype(jnp.int32) + has_behind.astype(jnp.int32))
-        start_halo(0, b)
+            pl.semaphore_wait(barrier, 2 + has_onward.astype(jnp.int32))
+        across(0, b).start()
     exchange_cols().start()
     for b in range(rows):
         exchange(b).start()
@@ -206,7 +186,7 @@
         re, im = reflected(*row_of(0, b), c_re[:, at], c_im[:, at])
         field[1, rows + b, 0:half] = re
         field[1, rows + b, half:full] = im
-        start_halo(1, b)
+        across(1, b).start()
     for b in range(rows):
         split_slot(1, rows + b)
 
@@ -236,14 +216,8 @@
     @pl.when(has_onward)
     def _():
         for l in range(2):
-            for b in range(relayed):
+            for b in range(rows):
                 along(l, b).wait_send()
-
-    @pl.when(has_behind)
-    def _():
-        for l in range(2):
-            for b in range(relayed, rows):
-                direct(l, b).wait_send()
 
     store.wait()
 
@@ -284,7 +258,7 @@
             pltpu.SMEM(block_cols.shape, jnp.int32),
             dma((rows,)), dma((1,)), dma((2,)), dma((1,)),
             dma((rows,)), dma((rows,)), dma((1,)), dma((1,)),
-            dma((2, rows)), dma((2, rows)), dma((2, rows)), dma((2, rows)), dma((2, rows)), dma((1,)),
+            dma((2, rows)), dma((2, rows)), dma((2, rows)), dma((2, rows)), dma((1,)),
         ],
         compiler_params=pltpu.CompilerParams(
             collective_id=0, has_side_effects=True, vmem_limit_bytes=63 * 1024 * 1024

time: 25 us -> 24 us (0.960)
  Pallas kernels: 23.2 us -> 22.2 us
    pallas_call x1, Pallas kernels: 23.2 us -> 22.2 us  [per_device(): pl.pallas_call(functools.partial(kernel, lat_count), out_shape=jax.ShapeD...]
where the time goes in v6:
time: 24 us; the launch traced here: 23.9 us
  Pallas kernels  22.2 us (92%)
  local copies, waits for them, and re-layouts  1.62 us (7%)
    pallas_call x1, Pallas kernels, per_device(): pl.pallas_call(functools.partial(kernel, lat_count), out_shape=jax.ShapeD...  22.2 us
    unnamed x1, local copies, waits for them, and re-layouts  1.62 us

profile of v6, /device:TPU:10, one launch (start us, length us, event | category | flops | bytes accessed | tf_op | source)
XLA Modules:
  0.0 23.9 jit_solution(932895784884007367)
XLA Ops:
  0.0 22.2 %shard_map.55 = f32[3,2,16,512]{3,2,1,0:T(8,128)} custom-call(f32[1,4,7,2,128,128]{5,4,3,2,1,0:T(8,128)} %blocks.1, s32[1,4,7]{2,1,0:T(4,128)} %cols_hbm.1, s32[1,4,7]{2,1,0:T(4,128)} %cols_hbm.1, f32[3,2,16,512]{3,2,1,0:T(8,128)} %sources.1, s32[1,512]{1,0:T(1,128)} %bitcast.1, f32[2,512]{1,0:T(2,128)} %coef.1), custom_call_target="tpu_custom_call" | custom-call | flops 1056964608 | bytes 4063232 | tf_op jit(solution)/shard_map/pallas_call | solution.py:235
  22.3 1.6 %copy.7 = f32[3,2,16,512]{3,2,1,0:T(8,128)} copy(f32[3,2,16,512]{3,2,1,0:T(8,128)} %shard_map.55) | data formatting | bytes 393216

commit v7 on v6

--- a/solution.py
+++ b/solution.py
@@ -141,6 +141,12 @@
         of_re, of_im = total[:half], total[half:]
         return of_re[:, :size] - of_im[:, size:], of_re[:, size:] + of_im[:, :size]
 
+    def store(b):
+        at = pl.ds(b * size, size)
+        return pltpu.make_async_copy(
+            final.at[:, :, :, at], out.at[:, :, :, at], store_o.at[b]
+        )
+
     c_re, c_im = coefficients(0)
     source_load.wait()
     for b in range(rows):
@@ -151,7 +157,8 @@
             field[0, rows + b, half + k * part:half + (k + 1) * part] = im
         if b == 0:
             pl.semaphore_wait(barrier, 2 + has_onward.astype(jnp.int32))
-        across(0, b).start()
+        if b < rows // 2:
+            across(0, b).start()
     exchange_cols().start()
     for b in range(rows):
         exchange(b).start()
@@ -161,6 +168,8 @@
     for b in range(rows):
         weight_loads[b].wait()
         split_row(depth, b)
+        if b < rows - rows // 2:
+            across(0, b + rows // 2).start()
         if b >= rows // 2:
             pass_on(0, b - rows // 2)
     early = rows // 2
@@ -204,8 +213,7 @@
         for k in range(panels):
             final[k, 0, :, at] = re[k * part:(k + 1) * part]
             final[k, 1, :, at] = im[k * part:(k + 1) * part]
-    store = pltpu.make_async_copy(final, out, store_o.at[0])
-    store.start()
+        store(b).start()
 
     exchange_cols().wait_send()
     for b in range(rows):
@@ -219,7 +227,8 @@
             for b in range(rows):
                 along(l, b).wait_send()
 
-    store.wait()
+    for b in range(rows):
+        store(b).wait()
 
 
 def per_device(sources, blocks, block_cols, refl_level, refl_coef):
@@ -258,7 +267,7 @@
             pltpu.SMEM(block_cols.shape, jnp.int32),
             dma((rows,)), dma((1,)), dma((2,)), dma((1,)),
             dma((rows,)), dma((rows,)), dma((1,)), dma((1,)),
-            dma((2, rows)), dma((2, rows)), dma((2, rows)), dma((2, rows)), dma((1,)),
+            dma((2, rows)), dma((2, rows)), dma((2, rows)), dma((2, rows)), dma((rows,)),
         ],
         compiler_params=pltpu.CompilerParams(
             collective_id=0, has_side_effects=True, vmem_limit_bytes=63 * 1024 * 1024

time: 24 us -> 24.1 us (level)
  no operation moved by 1% of the time
where the time goes in v7:
time: 24.1 us; the launch traced here: 23.9 us
  Pallas kernels  22.3 us (93%)
  local copies, waits for them, and re-layouts  1.62 us (7%)
    pallas_call x1, Pallas kernels, per_device(): pl.pallas_call(functools.partial(kernel, lat_count), out_shape=jax.ShapeD...  22.3 us
    unnamed x1, local copies, waits for them, and re-layouts  1.62 us

profile of v7, /device:TPU:10, one launch (start us, length us, event | category | flops | bytes accessed | tf_op | source)
XLA Modules:
  0.0 23.9 jit_solution(11449631396789890012)
XLA Ops:
  0.0 22.3 %shard_map.55 = f32[3,2,16,512]{3,2,1,0:T(8,128)} custom-call(f32[1,4,7,2,128,128]{5,4,3,2,1,0:T(8,128)} %blocks.1, s32[1,4,7]{2,1,0:T(4,128)} %cols_hbm.1, s32[1,4,7]{2,1,0:T(4,128)} %cols_hbm.1, f32[3,2,16,512]{3,2,1,0:T(8,128)} %sources.1, s32[1,512]{1,0:T(1,128)} %bitcast.1, f32[2,512]{1,0:T(2,128)} %coef.1), custom_call_target="tpu_custom_call" | custom-call | flops 1056964608 | bytes 4063232 | tf_op jit(solution)/shard_map/pallas_call | solution.py:244
  22.3 1.6 %copy.7 = f32[3,2,16,512]{3,2,1,0:T(8,128)} copy(f32[3,2,16,512]{3,2,1,0:T(8,128)} %shard_map.55) | data formatting | bytes 393216

commit v8 on v7

--- a/solution.py
+++ b/solution.py
@@ -172,18 +172,15 @@
             across(0, b + rows // 2).start()
         if b >= rows // 2:
             pass_on(0, b - rows // 2)
-    early = rows // 2
     for b in range(rows - rows // 2, rows):
         pass_on(0, b)
-    for b in range(early):
-        split_received(b)
     exchange_cols().wait_recv()
     listed = pltpu.make_async_copy(cols_in, cols_other, load_c.at[0])
     listed.start()
 
     @pl.when(depth == 1)
     def _():
-        for b in range(early, rows):
+        for b in range(rows):
             split_received(b)
 
     listed.wait()
@@ -201,7 +198,7 @@
 
     @pl.when(depth == 0)
     def _():
-        for b in range(early, rows):
+        for b in range(rows):
             split_received(b)
 
     for b in range(rows):

time: 24.1 us -> 24.1 us (level)
  no operation moved by 1% of the time
where the time goes in v8:
time: 24.1 us; the launch traced here: 23.9 us
  Pallas kernels  22.3 us (93%)
  local copies, waits for them, and re-layouts  1.62 us (7%)
    pallas_call x1, Pallas kernels, per_device(): pl.pallas_call(functools.partial(kernel, lat_count), out_shape=jax.ShapeD...  22.3 us
    unnamed x1, local copies, waits for them, and re-layouts  1.62 us

profile of v8, /device:TPU:10, one launch (start us, length us, event | category | flops | bytes accessed | tf_op | source)
XLA Modules:
  0.0 23.9 jit_solution(8268958863933356223)
XLA Ops:
  0.0 22.3 %shard_map.55 = f32[3,2,16,512]{3,2,1,0:T(8,128)} custom-call(f32[1,4,7,2,128,128]{5,4,3,2,1,0:T(8,128)} %blocks.1, s32[1,4,7]{2,1,0:T(4,128)} %cols_hbm.1, s32[1,4,7]{2,1,0:T(4,128)} %cols_hbm.1, f32[3,2,16,512]{3,2,1,0:T(8,128)} %sources.1, s32[1,512]{1,0:T(1,128)} %bitcast.1, f32[2,512]{1,0:T(2,128)} %coef.1), custom_call_target="tpu_custom_call" | custom-call | flops 1056964608 | bytes 4063232 | tf_op jit(solution)/shard_map/pallas_call | solution.py:241
  22.3 1.6 %copy.7 = f32[3,2,16,512]{3,2,1,0:T(8,128)} copy(f32[3,2,16,512]{3,2,1,0:T(8,128)} %shard_map.55) | data formatting | bytes 393216
